TPU v7x, 128 devices: a whole 4x4x4 slice. The times are simulated.
128 devices in a mesh: section: 2 (over core), et: 2 (over x_hi), dp: 32 (over z, y, x_lo).
Axes of the slice: x: 4 (x_hi: 2, x_lo: 2; x = x_hi * 2 + x_lo), y: 4, z: 4, core: 2. Of those that a mesh axis runs over, the one named last changes fastest.
Arguments:
- layer_inputs: bfloat16 [2, 1, 8192, 2048], P('section', None, ('dp', 'et')), may hold values from -6 to 6
- out_grad: bfloat16 [1, 8192, 2048], P(None, ('dp', 'et')), may hold values from -6 to 6
- w_gate: bfloat16 [2, 2048, 7168], P('section', None, 'et'), may hold values from -0.125 to 0.125
- w_up: bfloat16 [2, 2048, 7168], P('section', None, 'et'), may hold values from -0.125 to 0.125
- w_down: bfloat16 [2, 2048, 7168], P('section', None, 'et'), may hold values from -0.0625 to 0.0625
- slot_token: int32 [2, 1, 4096], P('section', None, 'dp'), may hold values from -1 to 255, as said below
- slot_gate: float32 [2, 1, 4096], P('section', None, 'dp'), may hold values from 0.1 to 0.9
Outputs:
- in_grad: bfloat16 [2, 1, 8192, 2048], P('section', None, ('dp', 'et'))
- gate_w_grad: bfloat16 [2, 2048, 7168], P('section', 'dp', 'et')
- up_w_grad: bfloat16 [2, 2048, 7168], P('section', 'dp', 'et')
- down_w_grad: bfloat16 [2, 2048, 7168], P('section', 'dp', 'et')
- gate_value_grad: float32 [2, 1, 4096], P('section', None, 'dp')
Inputs may be any that keep to these rules, and one draw needn't show every extreme that they name: `slot_token`: each layout (one section, micro-batch and replica) holds distinct tokens of its replica in rising order in its first slots and -1 in the rest; from 64 to 128 slots are live, and in every draw some layout is full.
All inputs are finite; a program needn't handle non-finite values.
Results may differ from a plain program's by a relative error of at most 0.024.
Values may be sent and summed in bfloat16 or wider, within the bound.
A program may use at most 320 MiB of HBM per device.

v0:
```python
import jax
import jax.numpy as jnp
from jax import lax
from jax.experimental import pallas as pl
from jax.experimental.pallas import tpu as pltpu
from jax.sharding import PartitionSpec as P

BF = jnp.bfloat16
F32 = jnp.float32
NY, NZ, NX = 4, 4, 2
RING = 4
COLS = 256
MESH = pl.DeviceIdType.MESH


def dot(a, b):
    return jnp.dot(a, b, preferred_element_type=F32)


def dot_nt(a, b):
    return lax.dot_general(a, b, (((1,), (1,)), ((), ())), preferred_element_type=F32)


def body(
    slots_col, slots_row, gates_col, x_hbm, g_hbm, w1_hbm, w3_hbm, w2_hbm,
    in_grad, gate_out, up_out, down_out, value_out,
    w1, w3, w2, x_full, g_full, x_rows, g_rows, x_turned, s_turned,
    active_ref, slope_ref, right, left, rows_sum, rows_mine, rows_theirs, grads_both,
    value_mine, value_theirs,
    load_sem, w2_sem, local_sem, pair_send, pair_recv, hop_send, hop_recv,
    left_send, left_recv, right_send, right_recv, sum_send, sum_recv, x_send, x_recv, ready,
):
    section = lax.axis_index("section")
    et = lax.axis_index("et")
    dp = lax.axis_index("dp")
    z, y, x = dp // (NY * NX), (dp // NX) % NY, dp % NX
    slots_n = slots_row.shape[1]
    tok = x_full.shape[1]
    chunks = w1.shape[0]
    half = chunks // 2
    ring_w2 = w2.shape[0]
    width = w1.shape[1]

    def at_y(step):
        return (section, et, z * (NY * NX) + ((y + step) % NY) * NX + x)

    def at_z(step):
        return (section, et, ((z + step) % NZ) * (NY * NX) + y * NX + x)

    pair = (section, 1 - et, dp)
    sibling = (1 - section, et, dp)
    x_peer = (section, et, z * (NY * NX) + y * NX + (1 - x))
    gather_to = (at_y, at_z)
    reduce_to = (at_z, at_y)
    gather_pos = (y, z)
    reduce_pos = (z, y)

    def remote(src, dst, send, recv, device):
        return pltpu.make_async_remote_copy(
            src_ref=src, dst_ref=dst, send_sem=send, recv_sem=recv,
            device_id=device, device_id_type=MESH)

    def w_load(hbm, ref, c, sem):
        start = pl.multiple_of(c * COLS, COLS)
        return pltpu.make_async_copy(hbm.at[0, :, pl.ds(start, COLS)], ref, sem)

    x_load = pltpu.make_async_copy(x_hbm.at[0, 0], x_full.at[0], local_sem.at[0])
    g_load = pltpu.make_async_copy(g_hbm.at[0], g_full.at[0], local_sem.at[1])
    x_load.start()

    @pl.when(section == 1)
    def _():
        g_load.start()

    @pl.loop(0, chunks)
    def _(c):
        w_load(w1_hbm, w1.at[c], c, load_sem.at[0, c]).start()
        w_load(w3_hbm, w3.at[c], c, load_sem.at[1, c]).start()

    @pl.loop(0, ring_w2)
    def _(c):
        w_load(w2_hbm, w2.at[c], c, w2_sem.at[c]).start()

    barrier = pltpu.get_barrier_semaphore()
    peers = [pair, sibling, x_peer] + [at_y(k) for k in (1, 2, 3)] + [at_z(k) for k in (1, 2, 3)]
    for peer in peers:
        pl.semaphore_signal(barrier, inc=1, device_id=peer, device_id_type=MESH)
    pl.semaphore_wait(barrier, len(peers))

    x_swap = remote(x_hbm.at[0, 0], x_full.at[1], pair_send.at[0], pair_recv.at[0], pair)
    g_swap = remote(g_hbm.at[0], g_full.at[1], pair_send.at[1], pair_recv.at[1], pair)
    x_swap.start()

    @pl.when(section == 1)
    def _():
        g_swap.start()

    token = lax.broadcasted_iota(jnp.int32, (slots_n, 2 * tok), 1)
    token = token + jnp.where(token < tok, et * tok, -et * tok)
    pick = jnp.where(slots_col[...] == token, 1.0, 0.0).astype(BF)
    turned = lax.broadcasted_iota(jnp.int32, (tok, slots_n), 0)
    place = [
        jnp.where(slots_row[...] == turned + et * tok, 1.0, 0.0).astype(BF),
        jnp.where(slots_row[...] == turned + (1 - et) * tok, 1.0, 0.0).astype(BF),
    ]

    def select(both):
        return dot(pick[:, :tok], both[0]) + dot(pick[:, tok:], both[1])

    def turn(rows, into):
        for b in range(width // 128):
            block = rows[:, b * 128:(b + 1) * 128].astype(F32)
            into[b // 4, b % 4] = block.T.astype(BF)

    def deal(which, source):
        copies = []
        for h in range(2):
            own = source.at[:, gather_pos[h]] if h == 0 else source.at[gather_pos[h]]
            left[which, h, :, :, 0:128] = own[...]
            for k in (1, 2, 3):
                there = (gather_pos[h] + k) % RING
                src = source.at[:, there] if h == 0 else source.at[there]
                copy = remote(src, left.at[which, h, :, :, pl.ds(k * 128, 128)],
                              left_send.at[which, h, k - 1], left_recv.at[which, h, k - 1], gather_to[h](k))
                copy.start()
                copies.append(copy)
        return copies

    def spread(t):
        copies = []
        for h in range(2):
            for k in (2, 1, 3):
                copy = remote(right.at[t, pl.ds(half * h, half), pl.ds(0, slots_n), :],
                              right.at[t, pl.ds(half * h, half), pl.ds(k * slots_n, slots_n), :],
                              right_send.at[t, h, k - 1], right_recv.at[t, h, k - 1], gather_to[h](k))
                copy.start()
                copies.append(copy)
        return copies

    x_load.wait()
    x_swap.wait_recv()
    x_rows[...] = select(x_full).astype(BF)

    @pl.loop(0, chunks)
    def _(c):
        w_load(w1_hbm, w1.at[c], c, load_sem.at[0, c]).wait()
        w_load(w3_hbm, w3.at[c], c, load_sem.at[1, c]).wait()
        pre_gate = dot(x_rows[...], w1[c])
        pre_up = dot(x_rows[...], w3[c])
        sigma = jax.nn.sigmoid(pre_gate)
        active = pre_gate * sigma
        active_ref[c] = active
        slope_ref[c] = pre_up * sigma * (1.0 + pre_gate * (1.0 - sigma))
        right[0, c, 0:slots_n, :] = (active * pre_up).astype(BF)

    sent = spread(0)
    turn(x_rows[...], x_turned)
    sent += deal(0, x_turned)

    hops = [remote(grads_both.at[i], g_full.at[i], hop_send.at[i], hop_recv.at[i], sibling) for i in range(2)]

    @pl.when(section == 1)
    def _():
        g_load.wait()
        g_swap.wait_recv()

    @pl.when(section == 0)
    def _():
        hops[0].wait_recv()
        hops[1].wait_recv()

    g_rows[...] = select(g_full).astype(BF)
    rows_sum[...] = jnp.zeros_like(rows_sum)
    value_mine[...] = jnp.zeros_like(value_mine)
    gates = gates_col[...]

    @pl.loop(0, chunks)
    def _(c):
        slot = c % ring_w2
        w_load(w2_hbm, w2.at[slot], c, w2_sem.at[slot]).wait()
        back = dot(g_rows[...], w2[slot])

        @pl.when(c + ring_w2 < chunks)
        def _():
            w_load(w2_hbm, w2.at[slot], c + ring_w2, w2_sem.at[slot]).start()

        product = right[0, c, 0:slots_n, :].astype(F32) * back
        value_mine[...] += product[:, :128] + product[:, 128:]
        scaled = gates * back
        grad_gate = (scaled * slope_ref[c]).astype(BF)
        grad_up = (scaled * active_ref[c]).astype(BF)
        right[1, c, 0:slots_n, :] = grad_gate
        right[2, c, 0:slots_n, :] = grad_up
        rows_sum[...] += dot_nt(w1[c], grad_gate) + dot_nt(w3[c], grad_up)

    rows_mine[...] = rows_sum[...].astype(BF)
    rows_swap = remote(rows_mine, rows_theirs, pair_send.at[2], pair_recv.at[2], pair)
    value_swap = remote(value_mine, value_theirs, pair_send.at[3], pair_recv.at[3], pair)
    rows_swap.start()
    value_swap.start()

    for peer in peers[2:]:
        pl.semaphore_signal(ready, inc=1, device_id=peer, device_id_type=MESH)

    sent += spread(1)
    sent += spread(2)
    turn(gates * g_rows[...].astype(F32), s_turned)
    sent += deal(1, s_turned)

    rows_swap.wait_recv()

    def token_grads(i):
        step = 512
        for b in range(width // step):
            cols = slice(b * step, (b + 1) * step)
            added = dot_nt(place[i], rows_mine[cols, :]) + dot_nt(place[i], rows_theirs[cols, :])
            grads_both[i, :, cols] = (g_full[i, :, cols].astype(F32) + added).astype(BF)

    @pl.when(section == 1)
    def _():
        token_grads(1)
        hops[1].start()

    token_grads(0)

    @pl.when(section == 1)
    def _():
        hops[0].start()

    in_grad[0, 0] = grads_both[0]
    value_swap.wait_recv()
    value_out[0] = jnp.sum((value_mine[...] + value_theirs[...]).T, axis=0, keepdims=True)

    outs = (down_out, gate_out, up_out)
    block = RING * 128

    def left_wait(which):
        for h in range(2):
            for k in (1, 2, 3):
                remote(left.at[which, h, :, :, pl.ds(k * 128, 128)], left.at[which, h, :, :, pl.ds(k * 128, 128)],
                       left_send.at[which, h, k - 1], left_recv.at[which, h, k - 1], gather_to[h](k)).wait_recv()

    def multiply(t, h):
        for k in (1, 3, 2):
            part = right.at[t, pl.ds(half * h, half), pl.ds(k * slots_n, slots_n), :]
            remote(part, part, right_send.at[t, h, k - 1], right_recv.at[t, h, k - 1], gather_to[h](k)).wait_recv()
        which = 1 if t == 0 else 0

        @pl.loop(0, half)
        def _(n):
            c = half * h + n
            a = left[which, h].reshape(block, RING * slots_n)
            w1[c, t * block:(t + 1) * block, :] = dot(a, right[t, c]).astype(BF)

    def sum_copy(t, h, k):
        there = pl.multiple_of(t * block + ((reduce_pos[h] + k) % RING) * 128, 128)
        return remote(w1.at[pl.ds(half * h, half), pl.ds(there, 128), :],
                      w3.at[pl.ds(half * h, half), pl.ds(t * block + k * 128, 128), :],
                      sum_send.at[t, h, k - 1], sum_recv.at[t, h, k - 1], reduce_to[h](k))

    def reduce_start(t, h):
        copies = []
        for k in (2, 1, 3):
            copy = sum_copy(t, h, k)
            copy.start()
            copies.append(copy)
        return copies

    def total(t, h, c, side):
        here = pl.multiple_of(t * block + reduce_pos[h] * 128 + side * 64, 64)
        value = w1[c, pl.ds(here, 64), :].astype(F32)
        for k in (1, 2, 3):
            there = pl.multiple_of(t * block + k * 128 + side * 64, 64)
            value = value + w3[c, pl.ds(there, 64), :].astype(F32)
        return value

    def x_copy(t, h):
        at = (pl.ds(half * h, half), pl.ds(3 * block + t * 64, 64), slice(None))
        return remote(w1.at[at], w3.at[at], x_send.at[t, h], x_recv.at[t, h], x_peer)

    def reduce_end(t, h):
        for k in (1, 3, 2):
            sum_copy(t, h, k).wait_recv()

        @pl.loop(0, half)
        def _(n):
            c = half * h + n
            w1[c, 3 * block + t * 64:3 * block + (t + 1) * 64, :] = total(t, h, c, 1 - x).astype(BF)
        copy = x_copy(t, h)
        copy.start()
        return [copy]

    def finish(t, h):
        x_copy(t, h).wait_recv()
        for n in range(half):
            c = half * h + n
            arrived = w3[c, 3 * block + t * 64:3 * block + (t + 1) * 64, :].astype(F32)
            outs[t][0, :, c * COLS:(c + 1) * COLS] = ((total(t, h, c, x) + arrived) * (1.0 / 32.0)).astype(BF)

    left_wait(1)
    multiply(0, 0)
    pl.semaphore_wait(ready, len(peers) - 2)
    sent += reduce_start(0, 0)
    multiply(0, 1)
    sent += reduce_start(0, 1)
    left_wait(0)
    for h in range(2):
        multiply(1, h)
        sent += reduce_start(1, h)
    for h in range(2):
        sent += reduce_end(0, h)
    for h in range(2):
        multiply(2, h)
        sent += reduce_start(2, h)
    for h in range(2):
        sent += reduce_end(1, h)
    for h in range(2):
        finish(0, h)
    for h in range(2):
        sent += reduce_end(2, h)
    for t in (1, 2):
        for h in range(2):
            finish(t, h)

    for copy in sent:
        copy.wait_send()
    x_swap.wait_send()
    rows_swap.wait_send()
    value_swap.wait_send()

    @pl.when(section == 1)
    def _():
        g_swap.wait_send()
        hops[0].wait_send()
        hops[1].wait_send()


def per_device(layer_inputs, out_grad, w_gate, w_up, w_down, slot_token, slot_gate):
    tok, width = layer_inputs.shape[2:]
    hidden = w_gate.shape[2]
    slots_n = slot_token.shape[2]
    chunks = hidden // COLS
    rows_out = width // (NY * NZ * NX)
    vmem = pl.BlockSpec(memory_space=pltpu.VMEM)
    hbm = pl.BlockSpec(memory_space=pl.ANY)
    sem = pltpu.SemaphoreType.DMA
    grad = jax.ShapeDtypeStruct((1, rows_out, hidden), BF)
    return pl.pallas_call(
        body,
        out_shape=(
            jax.ShapeDtypeStruct((1, 1, tok, width), BF), grad, grad, grad,
            jax.ShapeDtypeStruct((1, 1, slots_n), F32),
        ),
        in_specs=[vmem, vmem, vmem, hbm, hbm, hbm, hbm, hbm],
        out_specs=(vmem,) * 5,
        scratch_shapes=[
            pltpu.VMEM((chunks, width, COLS), BF),
            pltpu.VMEM((chunks, width, COLS), BF),
            pltpu.VMEM((chunks // 2, width, COLS), BF),
            pltpu.VMEM((2, tok, width), BF),
            pltpu.VMEM((2, tok, width), BF),
            pltpu.VMEM((slots_n, width), BF),
            pltpu.VMEM((slots_n, width), BF),
            pltpu.VMEM((RING, RING, 128, slots_n), BF),
            pltpu.VMEM((RING, RING, 128, slots_n), BF),
            pltpu.VMEM((chunks, slots_n, COLS), F32),
            pltpu.VMEM((chunks, slots_n, COLS), F32),
            pltpu.VMEM((3, chunks, RING * slots_n, COLS), BF),
            pltpu.VMEM((2, 2, RING, 128, RING * slots_n), BF),
            pltpu.VMEM((width, slots_n), F32),
            pltpu.VMEM((width, slots_n), BF),
            pltpu.VMEM((width, slots_n), BF),
            pltpu.VMEM((2, tok, width), BF),
            pltpu.VMEM((slots_n, 128), F32),
            pltpu.VMEM((slots_n, 128), F32),
            sem((2, chunks)), sem((chunks // 2,)), sem((2,)),
            sem((4,)), sem((4,)), sem((2,)), sem((2,)),
            sem((2, 2, 3)), sem((2, 2, 3)), sem((3, 2, 3)), sem((3, 2, 3)),
            sem((3, 2, 3)), sem((3, 2, 3)), sem((3, 2)), sem((3, 2)),
            pltpu.SemaphoreType.REGULAR,
        ],
        compiler_params=pltpu.CompilerParams(
            collective_id=0, has_side_effects=True, vmem_limit_bytes=63 * 1024 * 1024),
    )(
        slot_token.reshape(slots_n, 1), slot_token.reshape(1, slots_n), slot_gate.reshape(slots_n, 1),
        layer_inputs, out_grad, w_gate, w_up, w_down,
    )


def solution(mesh):
    placed = (
        P("section", None, ("dp", "et"), None),
        P(None, ("dp", "et"), None),
        P("section", None, "et"),
        P("section", None, "et"),
        P("section", None, "et"),
        P("section", None, "dp"),
        P("section", None, "dp"),
    )
    return jax.shard_map(
        per_device,
        mesh=mesh,
        in_specs=placed,
        out_specs=(
            P("section", None, ("dp", "et"), None),
            P("section", "dp", "et"),
            P("section", "dp", "et"),
            P("section", "dp", "et"),
            P("section", None, "dp"),
        ),
        check_vma=False,
    )
```

profile of v0, /device:TPU:0, one launch (start us, length us, event | category | flops | bytes accessed | tf_op | source)
XLA Modules:
  0.0 182.1 jit_solution(9441370583211646750)
XLA Ops:
  0.6 1.4 copy.13.gates_col
  2.0 1.4 copy.12.slots_col
  3.4 170.2 %shard_map.110 = (bf16[1,1,128,2048]{3,2,1,0:T(8,128)(2,1)}, bf16[1,64,3584]{2,1,0:T(8,128)(2,1)}, bf16[1,64,3584]{2,1,0:T(8,128)(2,1)}, bf16[1,64,3584]{2,1,0:T(8,128)(2,1)}, f32[1,1,128]{2,1,0:T(1,128)}) custom-call(s32[128,1]{1,0:T(8,128)} %copy.12.slots_col, s32[1,128]{1,0:T(1,128)} %bitcast.4, f32[128,1]{1,0:T(8,128)} %copy.13.gates_col, ...), custom_call_target="tpu_custom_call" | custom-call | tf_op jit(solution)/shard_map/pallas_call | solution.py:348
  173.7 1.9 %copy.19 = bf16[1,1,128,2048]{3,2,1,0:T(8,128)(2,1)} copy(bf16[1,1,128,2048]{3,2,1,0:T(8,128)(2,1)} %get-tuple-element.10) | data formatting | bytes 1048576
  175.5 1.8 copy.20
  177.4 1.8 copy.21
  179.2 1.8 copy.22
  181.0 1.1 copy.23
where the time goes:
time: 184 us; the launch traced here: 182 us
  Pallas kernels  170 us (92%)
  local copies, waits for them, and re-layouts  11.2 us (6%)
    pallas_call x1, Pallas kernels, per_device(): pl.pallas_call(body, out_shape=(jax.ShapeDtypeStruct((1, 1, tok, width),...  170 us
    unnamed x5, local copies, waits for them, and re-layouts  8.4 us

commit v1 on v0

v1 whole, which is shorter than its diff:
```python
import jax
import jax.numpy as jnp
from jax import lax
from jax.experimental import pallas as pl
from jax.experimental.pallas import tpu as pltpu
from jax.sharding import PartitionSpec as P

BF = jnp.bfloat16
F32 = jnp.float32
NY, NZ, NX = 4, 4, 2
RING = 4
COLS = 256
MESH = pl.DeviceIdType.MESH


def dot(a, b):
    return jnp.dot(a, b, preferred_element_type=F32)


def dot_nt(a, b):
    return lax.dot_general(a, b, (((1,), (1,)), ((), ())), preferred_element_type=F32)


def body(
    slots_ref, gates_ref, x_hbm, g_hbm, w1_hbm, w3_hbm, w2_hbm,
    in_grad, gate_out, up_out, down_out, value_out,
    w1, w3, w2, x_full, g_full, x_rows, g_rows, x_turned, s_turned,
    active_ref, slope_ref, right, left, rows_mine, rows_theirs, grads_both,
    value_mine, value_theirs,
    load_sem, w2_sem, local_sem, pair_send, pair_recv, rows_send, rows_recv, hop_send, hop_recv,
    left_send, left_recv, right_send, right_recv, far_send, far_recv, sum_send, sum_recv, x_send, x_recv,
    ready, turn_sem,
):
    section = lax.axis_index("section")
    et = lax.axis_index("et")
    dp = lax.axis_index("dp")
    z, y, x = dp // (NY * NX), (dp // NX) % NY, dp % NX
    slots_n = slots_ref.shape[2]
    tok = x_full.shape[1]
    chunks = w1.shape[0]
    half = chunks // 2
    ring_w2 = w2.shape[0]
    width = w1.shape[1]
    part_of = ((0, (half + 1) // 2), ((half + 1) // 2, half // 2))
    step_a = 1 + 2 * section
    step_b = 3 - 2 * section
    steps = (step_a, step_b)

    def at_y(step):
        return (section, et, z * (NY * NX) + ((y + step) % NY) * NX + x)

    def at_z(step):
        return (section, et, ((z + step) % NZ) * (NY * NX) + y * NX + x)

    pair = (section, 1 - et, dp)
    sibling = (1 - section, et, dp)
    x_peer = (section, et, z * (NY * NX) + y * NX + (1 - x))
    gather_to = (at_y, at_z)
    reduce_to = (at_z, at_y)
    gather_pos = (y, z)
    reduce_pos = (z, y)

    def remote(src, dst, send, recv, device):
        return pltpu.make_async_remote_copy(
            src_ref=src, dst_ref=dst, send_sem=send, recv_sem=recv,
            device_id=device, device_id_type=MESH)

    def w_load(hbm, ref, c, sem):
        start = pl.multiple_of(c * COLS, COLS)
        return pltpu.make_async_copy(hbm.at[0, :, pl.ds(start, COLS)], ref, sem)

    x_load = pltpu.make_async_copy(x_hbm.at[0, 0], x_full.at[0], local_sem.at[0])
    g_load = pltpu.make_async_copy(g_hbm.at[0], g_full.at[0], local_sem.at[1])
    x_load.start()

    @pl.when(section == 1)
    def _():
        g_load.start()

    @pl.loop(0, chunks)
    def _(c):
        w_load(w1_hbm, w1.at[c], c, load_sem.at[0, c]).start()
        w_load(w3_hbm, w3.at[c], c, load_sem.at[1, c]).start()

    @pl.loop(0, ring_w2)
    def _(c):
        w_load(w2_hbm, w2.at[c], c, w2_sem.at[c]).start()

    barrier = pltpu.get_barrier_semaphore()
    near = [x_peer] + [at_y(k) for k in (1, 3)] + [at_z(k) for k in (1, 3)]
    peers = [pair, sibling, at_y(2), at_z(2)] + near
    for peer in peers:
        pl.semaphore_signal(barrier, inc=1, device_id=peer, device_id_type=MESH)
    pl.semaphore_wait(barrier, len(peers))

    x_swap = remote(x_hbm.at[0, 0], x_full.at[1], pair_send.at[0], pair_recv.at[0], pair)
    g_swap = remote(g_hbm.at[0], g_full.at[1], pair_send.at[1], pair_recv.at[1], pair)

    @pl.when(section == 0)
    def _():
        pl.semaphore_wait(turn_sem, 1)

    x_swap.start()

    @pl.when(section == 1)
    def _():
        x_swap.wait_send()
        g_swap.start()

    def down_rows(row):
        return jnp.broadcast_to(row.astype(F32), (slots_n, slots_n)).T

    offsets = (et * tok, (1 - et) * tok)
    slot_rows = down_rows(slots_ref[0]).astype(jnp.int32)
    across = lax.broadcasted_iota(jnp.int32, (slots_n, tok), 1)
    pick = [jnp.where(slot_rows == across + o, 1.0, 0.0).astype(BF) for o in offsets]
    along = lax.broadcasted_iota(jnp.int32, (tok, slots_n), 0)
    place = [jnp.where(slots_ref[0] == along + o, 1.0, 0.0).astype(BF) for o in offsets]

    def deal(which, source):
        copies = []
        for h in range(2):
            def share(pos):
                return source.at[:, pos] if h == 0 else source.at[pos]
            left[which, h, :, :, 0:128] = share(gather_pos[h])[...]
            for k, step in ((2, 2), (1, step_a), (3, step_b)):
                copy = remote(share((gather_pos[h] + step) % RING), left.at[which, h, :, :, pl.ds(k * 128, 128)],
                              left_send.at[which, h, k - 1], left_recv.at[which, h, k - 1], gather_to[h](step))
                copy.start()
                copies.append(copy)
        return copies

    def piece(t, h, p, k):
        start, count = part_of[p]
        return right.at[t, pl.ds(half * h + start, count), pl.ds(k * slots_n, slots_n), :]

    def spread_copy(t, h, d, p):
        return remote(piece(t, h, p, 0), piece(t, h, p, 1 + 2 * d),
                      right_send.at[t, h, d, p], right_recv.at[t, h, d, p], gather_to[h](steps[d]))

    def pass_copy(t, h, d):
        return remote(piece(t, h, d, 1 + 2 * d), piece(t, h, d, 2),
                      far_send.at[t, h, d], far_recv.at[t, h, d], gather_to[h](steps[d]))

    def spread(t):
        copies = []
        for d, p in ((0, 0), (1, 1), (0, 1), (1, 0)):
            for h in range(2):
                copy = spread_copy(t, h, d, p)
                copy.start()
                copies.append(copy)
        return copies

    def pass_on(t):
        for h in range(2):
            for d in range(2):
                spread_copy(t, h, d, d).wait_recv()
                pass_copy(t, h, d).start()

    x_load.wait()
    x_swap.wait_recv()
    for b in range(width // 128):
        cols = slice(b * 128, (b + 1) * 128)
        picked = dot(pick[0], x_full[0, :, cols]) + dot(pick[1], x_full[1, :, cols])
        x_rows[:, cols] = picked.astype(BF)
        x_turned[b // 4, b % 4] = picked.T.astype(BF)
    sent = deal(0, x_turned)

    @pl.loop(0, chunks)
    def _(c):
        w_load(w1_hbm, w1.at[c], c, load_sem.at[0, c]).wait()
        w_load(w3_hbm, w3.at[c], c, load_sem.at[1, c]).wait()
        pre_gate = dot(x_rows[...], w1[c])
        pre_up = dot(x_rows[...], w3[c])
        sigma = jax.nn.sigmoid(pre_gate)
        active = pre_gate * sigma
        active_ref[c] = active
        slope_ref[c] = pre_up * sigma * (1.0 + pre_gate * (1.0 - sigma))
        right[0, c, 0:slots_n, :] = (active * pre_up).astype(BF)

    sent += spread(0)

    blocks = grads_both.shape[0]
    step = width // blocks

    def hop(b):
        return remote(grads_both.at[b], g_full.at[:, :, pl.ds(b * step, step)],
                      hop_send.at[b], hop_recv.at[b], sibling)

    @pl.when(section == 1)
    def _():
        g_swap.wait_send()
        pl.semaphore_signal(turn_sem, inc=1, device_id=sibling, device_id_type=MESH)
        g_load.wait()
        g_swap.wait_recv()

    @pl.when(section == 0)
    def _():
        pass_on(0)

    for b in range(blocks):
        cols = slice(b * step, (b + 1) * step)

        @pl.when(section == 0)
        def _():
            hop(b).wait_recv()

        g_rows[:, cols] = (dot(pick[0], g_full[0, :, cols]) + dot(pick[1], g_full[1, :, cols])).astype(BF)

    value_mine[...] = jnp.zeros_like(value_mine)
    gate_block = down_rows(gates_ref[0])
    gates = jnp.concatenate([gate_block] * (COLS // 128), axis=1)

    @pl.loop(0, chunks)
    def _(c):
        slot = c % ring_w2
        w_load(w2_hbm, w2.at[slot], c, w2_sem.at[slot]).wait()
        back = dot(g_rows[...], w2[slot])

        @pl.when(c + ring_w2 < chunks)
        def _():
            w_load(w2_hbm, w2.at[slot], c + ring_w2, w2_sem.at[slot]).start()

        product = right[0, c, 0:slots_n, :].astype(F32) * back
        value_mine[...] += product[:, :128] + product[:, 128:]
        scaled = gates * back
        right[1, c, 0:slots_n, :] = (scaled * slope_ref[c]).astype(BF)
        right[2, c, 0:slots_n, :] = (scaled * active_ref[c]).astype(BF)

    sent += spread(1)
    sent += spread(2)
    value_swap = remote(value_mine, value_theirs, pair_send.at[2], pair_recv.at[2], pair)
    value_swap.start()

    def rows_swap(b):
        return remote(rows_mine.at[b], rows_theirs.at[b], rows_send.at[b], rows_recv.at[b], pair)

    @pl.loop(0, blocks)
    def _(b):
        at = pl.ds(pl.multiple_of(b * step, step), step)
        total_rows = jnp.zeros((step, slots_n), F32)
        for c in range(chunks):
            total_rows = (total_rows + dot_nt(w1[c, at, :], right[1, c, 0:slots_n, :])
                          + dot_nt(w3[c, at, :], right[2, c, 0:slots_n, :]))
        rows_mine[b] = total_rows.astype(BF)
        rows_swap(b).start()

    for peer in near:
        pl.semaphore_signal(ready, inc=1, device_id=peer, device_id_type=MESH)

    @pl.when(section == 1)
    def _():
        pass_on(0)

    for b in range(width // 128):
        cols = slice(b * 128, (b + 1) * 128)
        s_turned[b // 4, b % 4] = (gate_block * g_rows[:, cols].astype(F32)).T.astype(BF)
    sent += deal(1, s_turned)

    for b in range(blocks):
        rows_swap(b).wait_recv()
        cols = slice(b * step, (b + 1) * step)

        def token_grads(i):
            added = dot_nt(place[i], rows_mine[b]) + dot_nt(place[i], rows_theirs[b])
            grads_both[b, i] = (g_full[i, :, cols].astype(F32) + added).astype(BF)

        token_grads(0)

        @pl.when(section == 1)
        def _():
            token_grads(1)
            hop(b).start()

        in_grad[0, 0, :, cols] = grads_both[b, 0]

    outs = (down_out, gate_out, up_out)
    block = RING * 128

    def left_wait(which):
        for h in range(2):
            for k, step in ((1, step_a), (3, step_b), (2, 2)):
                there = left.at[which, h, :, :, pl.ds(k * 128, 128)]
                remote(there, there, left_send.at[which, h, k - 1], left_recv.at[which, h, k - 1],
                       gather_to[h](step)).wait_recv()

    def multiply(t, h):
        for d in range(2):
            spread_copy(t, h, d, 1 - d).wait_recv()
        for d in range(2):
            pass_copy(t, h, d).wait_recv()
        which = 1 if t == 0 else 0

        @pl.loop(0, half)
        def _(n):
            c = half * h + n
            a = left[which, h].reshape(block, RING * slots_n)
            w1[c, t * block:(t + 1) * block, :] = dot(a, right[t, c]).astype(BF)

    def part_at(t, h, p, row):
        start, count = part_of[p]
        return (pl.ds(half * h + start, count), pl.ds(pl.multiple_of(t * block + row * 128, 128), 128), slice(None))

    def of_block(t, h, p, step):
        return part_at(t, h, p, (reduce_pos[h] + step) % RING)

    def far_sum(t, h, d):
        return remote(w1.at[of_block(t, h, d, 2)], w3.at[part_at(t, h, d, 2)],
                      sum_send.at[t, h, 0, d], sum_recv.at[t, h, 0, d], reduce_to[h](steps[d]))

    def near_sum(t, h, d, p):
        return remote(w1.at[of_block(t, h, p, steps[d])], w3.at[part_at(t, h, p, 1 + 2 * d)],
                      sum_send.at[t, h, 1 + p, d], sum_recv.at[t, h, 1 + p, d], reduce_to[h](steps[d]))

    def reduce_start(t, h):
        copies = [far_sum(t, h, d) for d in range(2)] + [near_sum(t, h, d, 1 - d) for d in range(2)]
        for copy in copies:
            copy.start()
        return copies

    def merge(t, h):
        copies = []
        for d in range(2):
            far_sum(t, h, d).wait_recv()
            here = of_block(t, h, d, steps[d])
            w1[here] = (w1[here].astype(F32) + w3[part_at(t, h, d, 2)].astype(F32)).astype(BF)
            copy = near_sum(t, h, d, d)
            copy.start()
            copies.append(copy)
        return copies

    def total(t, h, c, side):
        here = pl.multiple_of(t * block + reduce_pos[h] * 128 + side * 64, 64)
        value = w1[c, pl.ds(here, 64), :].astype(F32)
        for k in (1, 3):
            there = pl.multiple_of(t * block + k * 128 + side * 64, 64)
            value = value + w3[c, pl.ds(there, 64), :].astype(F32)
        return value

    def x_copy(t, h):
        at = (pl.ds(half * h, half), pl.ds(3 * block + t * 64, 64), slice(None))
        return remote(w1.at[at], w3.at[at], x_send.at[t, h], x_recv.at[t, h], x_peer)

    def reduce_end(t, h):
        for d in range(2):
            for p in range(2):
                near_sum(t, h, d, p).wait_recv()

        @pl.loop(0, half)
        def _(n):
            c = half * h + n
            w1[c, 3 * block + t * 64:3 * block + (t + 1) * 64, :] = total(t, h, c, 1 - x).astype(BF)
        copy = x_copy(t, h)
        copy.start()
        return [copy]

    def finish(t, h):
        x_copy(t, h).wait_recv()
        for n in range(half):
            c = half * h + n
            arrived = w3[c, 3 * block + t * 64:3 * block + (t + 1) * 64, :].astype(F32)
            outs[t][0, :, c * COLS:(c + 1) * COLS] = ((total(t, h, c, x) + arrived) * (1.0 / 32.0)).astype(BF)

    pass_on(1)
    left_wait(1)
    multiply(0, 0)
    pass_on(2)
    multiply(0, 1)
    pl.semaphore_wait(ready, len(near))
    sent += reduce_start(0, 0)
    sent += reduce_start(0, 1)
    left_wait(0)
    for t in (1, 2):
        for h in range(2):
            multiply(t, h)
            sent += reduce_start(t, h)
            sent += merge(t - 1, h)
    for h in range(2):
        sent += reduce_end(0, h)
    for h in range(2):
        sent += merge(2, h)
    for h in range(2):
        sent += reduce_end(1, h)
    value_swap.wait_recv()
    value_out[0] = jnp.sum((value_mine[...] + value_theirs[...]).T, axis=0, keepdims=True)
    for h in range(2):
        finish(0, h)
    for h in range(2):
        sent += reduce_end(2, h)
    for t in (1, 2):
        for h in range(2):
            finish(t, h)

    for copy in sent:
        copy.wait_send()
    for t in range(3):
        for h in range(2):
            for d in range(2):
                pass_copy(t, h, d).wait_send()
    for b in range(blocks):
        rows_swap(b).wait_send()
    value_swap.wait_send()

    @pl.when(section == 0)
    def _():
        x_swap.wait_send()

    @pl.when(section == 1)
    def _():
        for b in range(blocks):
            hop(b).wait_send()


def hand_out(*refs):
    sources, targets, sems = refs[:5], refs[5:10], refs[10]
    copies = [pltpu.make_async_copy(sources[i], targets[i], sems.at[i]) for i in range(5)]
    for copy in copies:
        copy.start()
    for copy in copies:
        copy.wait()


def per_device(layer_inputs, out_grad, w_gate, w_up, w_down, slot_token, slot_gate):
    tok, width = layer_inputs.shape[2:]
    hidden = w_gate.shape[2]
    slots_n = slot_token.shape[2]
    chunks = hidden // COLS
    rows_out = width // (NY * NZ * NX)
    vmem = pl.BlockSpec(memory_space=pltpu.VMEM)
    hbm = pl.BlockSpec(memory_space=pl.ANY)
    sem = pltpu.SemaphoreType.DMA
    grad = jax.ShapeDtypeStruct((1, rows_out, hidden), BF)
    shapes = (
        jax.ShapeDtypeStruct((1, 1, tok, width), BF), grad, grad, grad,
        jax.ShapeDtypeStruct((1, 1, slots_n), F32),
    )
    made = pl.pallas_call(
        body,
        out_shape=shapes,
        in_specs=[vmem, vmem, hbm, hbm, hbm, hbm, hbm],
        out_specs=(vmem,) * 5,
        scratch_shapes=[
            pltpu.VMEM((chunks, width, COLS), BF),
            pltpu.VMEM((chunks, width, COLS), BF),
            pltpu.VMEM((chunks // 2, width, COLS), BF),
            pltpu.VMEM((2, tok, width), BF),
            pltpu.VMEM((2, tok, width), BF),
            pltpu.VMEM((slots_n, width), BF),
            pltpu.VMEM((slots_n, width), BF),
            pltpu.VMEM((RING, RING, 128, slots_n), BF),
            pltpu.VMEM((RING, RING, 128, slots_n), BF),
            pltpu.VMEM((chunks, slots_n, COLS), F32),
            pltpu.VMEM((chunks, slots_n, COLS), F32),
            pltpu.VMEM((3, chunks, RING * slots_n, COLS), BF),
            pltpu.VMEM((2, 2, RING, 128, RING * slots_n), BF),
            pltpu.VMEM((4, width // 4, slots_n), BF),
            pltpu.VMEM((4, width // 4, slots_n), BF),
            pltpu.VMEM((4, 2, tok, width // 4), BF),
            pltpu.VMEM((slots_n, 128), F32),
            pltpu.VMEM((slots_n, 128), F32),
            sem((2, chunks)), sem((chunks // 2,)), sem((2,)),
            sem((3,)), sem((3,)), sem((4,)), sem((4,)), sem((4,)), sem((4,)),
            sem((2, 2, 3)), sem((2, 2, 3)), sem((3, 2, 2, 2)), sem((3, 2, 2, 2)), sem((3, 2, 2)), sem((3, 2, 2)),
            sem((3, 2, 3, 2)), sem((3, 2, 3, 2)), sem((3, 2)), sem((3, 2)),
            pltpu.SemaphoreType.REGULAR, pltpu.SemaphoreType.REGULAR,
        ],
        compiler_params=pltpu.CompilerParams(
            collective_id=0, has_side_effects=True, vmem_limit_bytes=63 * 1024 * 1024),
    )(slot_token, slot_gate, layer_inputs, out_grad, w_gate, w_up, w_down)
    return pl.pallas_call(
        hand_out,
        out_shape=shapes,
        in_specs=[vmem] * 5,
        out_specs=(hbm,) * 5,
        scratch_shapes=[sem((5,))],
    )(*made)


def solution(mesh):
    placed = (
        P("section", None, ("dp", "et"), None),
        P(None, ("dp", "et"), None),
        P("section", None, "et"),
        P("section", None, "et"),
        P("section", None, "et"),
        P("section", None, "dp"),
        P("section", None, "dp"),
    )
    return jax.shard_map(
        per_device,
        mesh=mesh,
        in_specs=placed,
        out_specs=(
            P("section", None, ("dp", "et"), None),
            P("section", "dp", "et"),
            P("section", "dp", "et"),
            P("section", "dp", "et"),
            P("section", None, "dp"),
        ),
        check_vma=False,
    )
```

time: 184 us -> 140 us (0.76)
  Pallas kernels: 170 us -> 139 us
  local copies, waits for them, and re-layouts: 11.2 us -> 0 us
    pallas_call x1 -> x2, Pallas kernels: 170 us -> 139 us  [the longest x1 136 us: per_device(): pl.pallas_call(body, out_shape=shapes, in_specs=[vmem, vmem, hbm, hbm, hb...]
    unnamed x5 -> x0, local copies, waits for them, and re-layouts: 8.4 us -> none
    reshape x2 -> x0, local copies, waits for them, and re-layouts: 2.78 us -> none  [the longest x1 1.39 us: per_device(): slot_gate.reshape(slots_n, 1)]
where the time goes in v1:
time: 140 us
  Pallas kernels  139 us (99%)
    pallas_call x1, Pallas kernels, per_device(): pl.pallas_call(body, out_shape=shapes, in_specs=[vmem, vmem, hbm, hbm, hb...  136 us

profile of v1, /device:TPU:0, one launch (start us, length us, event | category | flops | bytes accessed | tf_op | source)
XLA Modules:
  0.0 139.6 jit_solution(15186156092375592314)
XLA Ops:
  0.6 136.2 %shard_map.110 = (bf16[1,1,128,2048]{3,2,1,0:T(8,128)(2,1)}, bf16[1,64,3584]{2,1,0:T(8,128)(2,1)}, bf16[1,64,3584]{2,1,0:T(8,128)(2,1)}, bf16[1,64,3584]{2,1,0:T(8,128)(2,1)}, f32[1,1,128]{2,1,0:T(1,128)}) custom-call(s32[1,1,128]{2,1,0:T(1,128)} %slots_ref.1, f32[1,1,128]{2,1,0:T(1,128)} %gates_ref.1, bf16[1,1,128,2048]{3,2,1,0:T(8,128)(2,1)} %x_hbm.1, ...), custom_call_target="tpu_custom_call" | custom-call | tf_op jit(solution)/shard_map/pallas_call | solution.py:437
  136.8 2.7 %shard_map.111 = (bf16[1,1,128,2048]{3,2,1,0:T(8,128)(2,1)}, bf16[1,64,3584]{2,1,0:T(8,128)(2,1)}, bf16[1,64,3584]{2,1,0:T(8,128)(2,1)}, bf16[1,64,3584]{2,1,0:T(8,128)(2,1)}, f32[1,1,128]{2,1,0:T(1,128)}) custom-call(bf16[1,1,128,2048]{3,2,1,0:T(8,128)(2,1)} %get-tuple-element.10.refs_0_, bf16[1,64,3584]{2,1,0:T(8,128)(2,1)} %get-tuple-element.11.refs_1_, ...), custom_call_target="tpu_custom_call" | custom-call | tf_op jit(solution)/shard_map/pallas_call | solution.py:470

commit v2 on v1

--- a/solution.py
+++ b/solution.py
@@ -10,6 +10,7 @@
 NY, NZ, NX = 4, 4, 2
 RING = 4
 COLS = 256
+W2_RING = 6
 MESH = pl.DeviceIdType.MESH
 
 
@@ -24,12 +25,11 @@
 def body(
     slots_ref, gates_ref, x_hbm, g_hbm, w1_hbm, w3_hbm, w2_hbm,
     in_grad, gate_out, up_out, down_out, value_out,
-    w1, w3, w2, x_full, g_full, x_rows, g_rows, x_turned, s_turned,
-    active_ref, slope_ref, right, left, rows_mine, rows_theirs, grads_both,
+    w1, w3, w2, x_full, g_full, g_rows, x_group, s_group,
+    right, left, rows_mine, rows_theirs, grads_both,
     value_mine, value_theirs,
     load_sem, w2_sem, local_sem, pair_send, pair_recv, rows_send, rows_recv, hop_send, hop_recv,
-    left_send, left_recv, right_send, right_recv, far_send, far_recv, sum_send, sum_recv, x_send, x_recv,
-    ready, turn_sem,
+    group_send, group_recv, far_send, far_recv, sum_send, sum_recv, x_send, x_recv, ready,
 ):
     section = lax.axis_index("section")
     et = lax.axis_index("et")
@@ -88,17 +88,13 @@
 
     barrier = pltpu.get_barrier_semaphore()
     near = [x_peer] + [at_y(k) for k in (1, 3)] + [at_z(k) for k in (1, 3)]
-    peers = [pair, sibling, at_y(2), at_z(2)] + near
+    peers = [pair, sibling] + near
     for peer in peers:
         pl.semaphore_signal(barrier, inc=1, device_id=peer, device_id_type=MESH)
     pl.semaphore_wait(barrier, len(peers))
 
     x_swap = remote(x_hbm.at[0, 0], x_full.at[1], pair_send.at[0], pair_recv.at[0], pair)
     g_swap = remote(g_hbm.at[0], g_full.at[1], pair_send.at[1], pair_recv.at[1], pair)
-
-    @pl.when(section == 0)
-    def _():
-        pl.semaphore_wait(turn_sem, 1)
 
     x_swap.start()
 
@@ -117,68 +113,86 @@
     along = lax.broadcasted_iota(jnp.int32, (tok, slots_n), 0)
     place = [jnp.where(slots_ref[0] == along + o, 1.0, 0.0).astype(BF) for o in offsets]
 
-    def deal(which, source):
+    groups = (x_group, s_group)
+    span = width // 2
+
+    def piece(which, h, p, k):
+        return groups[which].at[h, pl.ds(k * slots_n, slots_n), pl.ds(p * span, span)]
+
+    def spread_copy(which, h, d, p):
+        return remote(piece(which, h, p, 0), piece(which, h, p, 1 + 2 * d),
+                      group_send.at[which, h, d, p], group_recv.at[which, h, d, p], gather_to[h](steps[d]))
+
+    def pass_copy(which, h, d):
+        return remote(piece(which, h, d, 1 + 2 * d), piece(which, h, d, 2),
+                      far_send.at[which, h, d], far_recv.at[which, h, d], gather_to[h](steps[d]))
+
+    def spread(which):
         copies = []
-        for h in range(2):
-            def share(pos):
-                return source.at[:, pos] if h == 0 else source.at[pos]
-            left[which, h, :, :, 0:128] = share(gather_pos[h])[...]
-            for k, step in ((2, 2), (1, step_a), (3, step_b)):
-                copy = remote(share((gather_pos[h] + step) % RING), left.at[which, h, :, :, pl.ds(k * 128, 128)],
-                              left_send.at[which, h, k - 1], left_recv.at[which, h, k - 1], gather_to[h](step))
+        for d, p in ((0, 0), (1, 1), (0, 1), (1, 0)):
+            for h in range(2):
+                copy = spread_copy(which, h, d, p)
                 copy.start()
                 copies.append(copy)
         return copies
 
-    def piece(t, h, p, k):
-        start, count = part_of[p]
-        return right.at[t, pl.ds(half * h + start, count), pl.ds(k * slots_n, slots_n), :]
-
-    def spread_copy(t, h, d, p):
-        return remote(piece(t, h, p, 0), piece(t, h, p, 1 + 2 * d),
-                      right_send.at[t, h, d, p], right_recv.at[t, h, d, p], gather_to[h](steps[d]))
-
-    def pass_copy(t, h, d):
-        return remote(piece(t, h, d, 1 + 2 * d), piece(t, h, d, 2),
-                      far_send.at[t, h, d], far_recv.at[t, h, d], gather_to[h](steps[d]))
-
-    def spread(t):
-        copies = []
-        for d, p in ((0, 0), (1, 1), (0, 1), (1, 0)):
-            for h in range(2):
-                copy = spread_copy(t, h, d, p)
-                copy.start()
-                copies.append(copy)
-        return copies
-
-    def pass_on(t):
+    def pass_on(which):
         for h in range(2):
             for d in range(2):
-                spread_copy(t, h, d, d).wait_recv()
-                pass_copy(t, h, d).start()
+                spread_copy(which, h, d, d).wait_recv()
+                pass_copy(which, h, d).start()
+
+    def group_wait(which):
+        for h in range(2):
+            for d in range(2):
+                spread_copy(which, h, d, 1 - d).wait_recv()
+                pass_copy(which, h, d).wait_recv()
+
+    own = pl.ds(0, slots_n)
+    others = pl.ds(slots_n, (RING - 1) * slots_n)
+
+    def forward(c, rows, at):
+        pre_gate = dot(rows, w1[c])
+        pre_up = dot(rows, w3[c])
+        sigma = jax.nn.sigmoid(pre_gate)
+        active = pre_gate * sigma
+        right[0, c, at, :] = (active * pre_up).astype(BF)
+        right[1, c, at, :] = (pre_up * sigma * (1.0 + pre_gate * (1.0 - sigma))).astype(BF)
+        right[2, c, at, :] = active.astype(BF)
+
+    def forward_others():
+        group_wait(0)
+
+        @pl.loop(0, chunks)
+        def _(c):
+            forward(c, x_group[c // half, others, :], others)
+
+    def backward(c, scaled, at):
+        for t in (1, 2):
+            right[t, c, at, :] = (scaled * right[t, c, at, :].astype(F32)).astype(BF)
+
+    def w2_load(i):
+        return w_load(w2_hbm, w2.at[i % ring_w2], i % chunks, w2_sem.at[i % ring_w2])
+
+    def w2_next(i):
+        @pl.when(i + ring_w2 < 2 * chunks)
+        def _():
+            w2_load(i + ring_w2).start()
 
     x_load.wait()
     x_swap.wait_recv()
-    for b in range(width // 128):
-        cols = slice(b * 128, (b + 1) * 128)
-        picked = dot(pick[0], x_full[0, :, cols]) + dot(pick[1], x_full[1, :, cols])
-        x_rows[:, cols] = picked.astype(BF)
-        x_turned[b // 4, b % 4] = picked.T.astype(BF)
-    sent = deal(0, x_turned)
+    picked = (dot(pick[0], x_full[0]) + dot(pick[1], x_full[1])).astype(BF)
+    for h in range(2):
+        x_group[h, own, :] = picked
+    sent = spread(0)
 
     @pl.loop(0, chunks)
     def _(c):
         w_load(w1_hbm, w1.at[c], c, load_sem.at[0, c]).wait()
         w_load(w3_hbm, w3.at[c], c, load_sem.at[1, c]).wait()
-        pre_gate = dot(x_rows[...], w1[c])
-        pre_up = dot(x_rows[...], w3[c])
-        sigma = jax.nn.sigmoid(pre_gate)
-        active = pre_gate * sigma
-        active_ref[c] = active
-        slope_ref[c] = pre_up * sigma * (1.0 + pre_gate * (1.0 - sigma))
-        right[0, c, 0:slots_n, :] = (active * pre_up).astype(BF)
-
-    sent += spread(0)
+        forward(c, x_group[0, own, :], own)
+
+    pass_on(0)
 
     blocks = grads_both.shape[0]
     step = width // blocks
@@ -189,15 +203,15 @@
 
     @pl.when(section == 1)
     def _():
-        g_swap.wait_send()
-        pl.semaphore_signal(turn_sem, inc=1, device_id=sibling, device_id_type=MESH)
         g_load.wait()
         g_swap.wait_recv()
 
     @pl.when(section == 0)
     def _():
-        pass_on(0)
-
+        forward_others()
+
+    gate_block = down_rows(gates_ref[0])
+    gates = jnp.concatenate([gate_block] * (COLS // 128), axis=1)
     for b in range(blocks):
         cols = slice(b * step, (b + 1) * step)
 
@@ -205,30 +219,24 @@
         def _():
             hop(b).wait_recv()
 
-        g_rows[:, cols] = (dot(pick[0], g_full[0, :, cols]) + dot(pick[1], g_full[1, :, cols])).astype(BF)
-
+        rows = (dot(pick[0], g_full[0, :, cols]) + dot(pick[1], g_full[1, :, cols])).astype(BF)
+        g_rows[:, cols] = rows
+        scaled_rows = (jnp.concatenate([gate_block] * (step // 128), axis=1) * rows.astype(F32)).astype(BF)
+        for h in range(2):
+            s_group[h, own, cols] = scaled_rows
+
+    sent += spread(1)
     value_mine[...] = jnp.zeros_like(value_mine)
-    gate_block = down_rows(gates_ref[0])
-    gates = jnp.concatenate([gate_block] * (COLS // 128), axis=1)
 
     @pl.loop(0, chunks)
     def _(c):
-        slot = c % ring_w2
-        w_load(w2_hbm, w2.at[slot], c, w2_sem.at[slot]).wait()
-        back = dot(g_rows[...], w2[slot])
-
-        @pl.when(c + ring_w2 < chunks)
-        def _():
-            w_load(w2_hbm, w2.at[slot], c + ring_w2, w2_sem.at[slot]).start()
-
-        product = right[0, c, 0:slots_n, :].astype(F32) * back
+        w2_load(c).wait()
+        back = dot(g_rows[...], w2[c % ring_w2])
+        w2_next(c)
+        product = right[0, c, own, :].astype(F32) * back
         value_mine[...] += product[:, :128] + product[:, 128:]
-        scaled = gates * back
-        right[1, c, 0:slots_n, :] = (scaled * slope_ref[c]).astype(BF)
-        right[2, c, 0:slots_n, :] = (scaled * active_ref[c]).astype(BF)
-
-    sent += spread(1)
-    sent += spread(2)
+        backward(c, gates * back, own)
+
     value_swap = remote(value_mine, value_theirs, pair_send.at[2], pair_recv.at[2], pair)
     value_swap.start()
 
@@ -240,22 +248,12 @@
         at = pl.ds(pl.multiple_of(b * step, step), step)
         total_rows = jnp.zeros((step, slots_n), F32)
         for c in range(chunks):
-            total_rows = (total_rows + dot_nt(w1[c, at, :], right[1, c, 0:slots_n, :])
-                          + dot_nt(w3[c, at, :], right[2, c, 0:slots_n, :]))
+            total_rows = (total_rows + dot_nt(w1[c, at, :], right[1, c, own, :])
+                          + dot_nt(w3[c, at, :], right[2, c, own, :]))
         rows_mine[b] = total_rows.astype(BF)
         rows_swap(b).start()
 
-    for peer in near:
-        pl.semaphore_signal(ready, inc=1, device_id=peer, device_id_type=MESH)
-
-    @pl.when(section == 1)
-    def _():
-        pass_on(0)
-
-    for b in range(width // 128):
-        cols = slice(b * 128, (b + 1) * 128)
-        s_turned[b // 4, b % 4] = (gate_block * g_rows[:, cols].astype(F32)).T.astype(BF)
-    sent += deal(1, s_turned)
+    pass_on(1)
 
     for b in range(blocks):
         rows_swap(b).wait_recv()
@@ -277,25 +275,22 @@
     outs = (down_out, gate_out, up_out)
     block = RING * 128
 
-    def left_wait(which):
-        for h in range(2):
-            for k, step in ((1, step_a), (3, step_b), (2, 2)):
-                there = left.at[which, h, :, :, pl.ds(k * 128, 128)]
-                remote(there, there, left_send.at[which, h, k - 1], left_recv.at[which, h, k - 1],
-                       gather_to[h](step)).wait_recv()
+    def left_make(which):
+        for h in range(2):
+            for j in range(RING):
+                at = (j * RING + gather_pos[h]) if h == 0 else (gather_pos[h] * RING + j)
+                cols = pl.ds(pl.multiple_of(at * 128, 128), 128)
+                for k in range(RING):
+                    tile = groups[which][h, k * slots_n:(k + 1) * slots_n, cols].astype(F32)
+                    left[which, h, j * 128:(j + 1) * 128, k * slots_n:(k + 1) * slots_n] = tile.T.astype(BF)
 
     def multiply(t, h):
-        for d in range(2):
-            spread_copy(t, h, d, 1 - d).wait_recv()
-        for d in range(2):
-            pass_copy(t, h, d).wait_recv()
         which = 1 if t == 0 else 0
 
         @pl.loop(0, half)
         def _(n):
             c = half * h + n
-            a = left[which, h].reshape(block, RING * slots_n)
-            w1[c, t * block:(t + 1) * block, :] = dot(a, right[t, c]).astype(BF)
+            w1[c, t * block:(t + 1) * block, :] = dot(left[which, h], right[t, c]).astype(BF)
 
     def part_at(t, h, p, row):
         start, count = part_of[p]
@@ -361,15 +356,29 @@
             arrived = w3[c, 3 * block + t * 64:3 * block + (t + 1) * 64, :].astype(F32)
             outs[t][0, :, c * COLS:(c + 1) * COLS] = ((total(t, h, c, x) + arrived) * (1.0 / 32.0)).astype(BF)
 
-    pass_on(1)
-    left_wait(1)
+    @pl.when(section == 1)
+    def _():
+        forward_others()
+
+    for peer in near:
+        pl.semaphore_signal(ready, inc=1, device_id=peer, device_id_type=MESH)
+    group_wait(1)
+    left_make(1)
     multiply(0, 0)
-    pass_on(2)
-    multiply(0, 1)
     pl.semaphore_wait(ready, len(near))
     sent += reduce_start(0, 0)
+    multiply(0, 1)
     sent += reduce_start(0, 1)
-    left_wait(0)
+
+    @pl.loop(0, chunks)
+    def _(c):
+        i = chunks + c
+        w2_load(i).wait()
+        scaled = dot(s_group[c // half, others, :], w2[i % ring_w2])
+        w2_next(i)
+        backward(c, scaled, others)
+
+    left_make(0)
     for t in (1, 2):
         for h in range(2):
             multiply(t, h)
@@ -393,10 +402,10 @@
 
     for copy in sent:
         copy.wait_send()
-    for t in range(3):
+    for which in range(2):
         for h in range(2):
             for d in range(2):
-                pass_copy(t, h, d).wait_send()
+                pass_copy(which, h, d).wait_send()
     for b in range(blocks):
         rows_swap(b).wait_send()
     value_swap.wait_send()
@@ -407,6 +416,7 @@
 
     @pl.when(section == 1)
     def _():
+        g_swap.wait_send()
         for b in range(blocks):
             hop(b).wait_send()
 
@@ -442,27 +452,24 @@
         scratch_shapes=[
             pltpu.VMEM((chunks, width, COLS), BF),
             pltpu.VMEM((chunks, width, COLS), BF),
-            pltpu.VMEM((chunks // 2, width, COLS), BF),
+            pltpu.VMEM((W2_RING, width, COLS), BF),
             pltpu.VMEM((2, tok, width), BF),
             pltpu.VMEM((2, tok, width), BF),
             pltpu.VMEM((slots_n, width), BF),
-            pltpu.VMEM((slots_n, width), BF),
-            pltpu.VMEM((RING, RING, 128, slots_n), BF),
-            pltpu.VMEM((RING, RING, 128, slots_n), BF),
-            pltpu.VMEM((chunks, slots_n, COLS), F32),
-            pltpu.VMEM((chunks, slots_n, COLS), F32),
+            pltpu.VMEM((2, RING * slots_n, width), BF),
+            pltpu.VMEM((2, RING * slots_n, width), BF),
             pltpu.VMEM((3, chunks, RING * slots_n, COLS), BF),
-            pltpu.VMEM((2, 2, RING, 128, RING * slots_n), BF),
+            pltpu.VMEM((2, 2, RING * 128, RING * slots_n), BF),
             pltpu.VMEM((4, width // 4, slots_n), BF),
             pltpu.VMEM((4, width // 4, slots_n), BF),
             pltpu.VMEM((4, 2, tok, width // 4), BF),
             pltpu.VMEM((slots_n, 128), F32),
             pltpu.VMEM((slots_n, 128), F32),
-            sem((2, chunks)), sem((chunks // 2,)), sem((2,)),
+            sem((2, chunks)), sem((W2_RING,)), sem((2,)),
             sem((3,)), sem((3,)), sem((4,)), sem((4,)), sem((4,)), sem((4,)),
-            sem((2, 2, 3)), sem((2, 2, 3)), sem((3, 2, 2, 2)), sem((3, 2, 2, 2)), sem((3, 2, 2)), sem((3, 2, 2)),
+            sem((2, 2, 2, 2)), sem((2, 2, 2, 2)), sem((2, 2, 2)), sem((2, 2, 2)),
             sem((3, 2, 3, 2)), sem((3, 2, 3, 2)), sem((3, 2)), sem((3, 2)),
-            pltpu.SemaphoreType.REGULAR, pltpu.SemaphoreType.REGULAR,
+            pltpu.SemaphoreType.REGULAR,
         ],
         compiler_params=pltpu.CompilerParams(
             collective_id=0, has_side_effects=True, vmem_limit_bytes=63 * 1024 * 1024),

time: 140 us -> 133 us (0.950)
  Pallas kernels: 139 us -> 132 us
    pallas_call x1, Pallas kernels: 136 us -> 129 us  [per_device(): pl.pallas_call(body, out_shape=shapes, in_specs=[vmem, vmem, hbm, hbm, hb...]
where the time goes in v2:
time: 133 us
  Pallas kernels  132 us (99%)
    pallas_call x1, Pallas kernels, per_device(): pl.pallas_call(body, out_shape=shapes, in_specs=[vmem, vmem, hbm, hbm, hb...  129 us
    pallas_call x1, Pallas kernels, per_device(): pl.pallas_call(hand_out, out_shape=shapes, in_specs=[vmem] * 5, out_specs...  2.74 us

profile of v2, /device:TPU:0, one launch (start us, length us, event | category | flops | bytes accessed | tf_op | source)
XLA Modules:
  0.0 132.9 jit_solution(9036218178033869905)
XLA Ops:
  0.6 129.5 %shard_map.110 = (bf16[1,1,128,2048]{3,2,1,0:T(8,128)(2,1)}, bf16[1,64,3584]{2,1,0:T(8,128)(2,1)}, bf16[1,64,3584]{2,1,0:T(8,128)(2,1)}, bf16[1,64,3584]{2,1,0:T(8,128)(2,1)}, f32[1,1,128]{2,1,0:T(1,128)}) custom-call(s32[1,1,128]{2,1,0:T(1,128)} %slots_ref.1, f32[1,1,128]{2,1,0:T(1,128)} %gates_ref.1, bf16[1,1,128,2048]{3,2,1,0:T(8,128)(2,1)} %x_hbm.1, ...), custom_call_target="tpu_custom_call" | custom-call | tf_op jit(solution)/shard_map/pallas_call | solution.py:447
  130.1 2.7 %shard_map.111 = (bf16[1,1,128,2048]{3,2,1,0:T(8,128)(2,1)}, bf16[1,64,3584]{2,1,0:T(8,128)(2,1)}, bf16[1,64,3584]{2,1,0:T(8,128)(2,1)}, bf16[1,64,3584]{2,1,0:T(8,128)(2,1)}, f32[1,1,128]{2,1,0:T(1,128)}) custom-call(bf16[1,1,128,2048]{3,2,1,0:T(8,128)(2,1)} %get-tuple-element.10.refs_0_, bf16[1,64,3584]{2,1,0:T(8,128)(2,1)} %get-tuple-element.11.refs_1_, ...), custom_call_target="tpu_custom_call" | custom-call | tf_op jit(solution)/shard_map/pallas_call | solution.py:477

commit v3 on v2

--- a/solution.py
+++ b/solution.py
@@ -10,7 +10,7 @@
 NY, NZ, NX = 4, 4, 2
 RING = 4
 COLS = 256
-W2_RING = 6
+W2_RING = 5
 MESH = pl.DeviceIdType.MESH
 
 
@@ -26,10 +26,11 @@
     slots_ref, gates_ref, x_hbm, g_hbm, w1_hbm, w3_hbm, w2_hbm,
     in_grad, gate_out, up_out, down_out, value_out,
     w1, w3, w2, x_full, g_full, g_rows, x_group, s_group,
-    right, left, rows_mine, rows_theirs, grads_both,
+    x_turned, s_turned, right, left, rows_mine, rows_theirs, grads_both,
     value_mine, value_theirs,
     load_sem, w2_sem, local_sem, pair_send, pair_recv, rows_send, rows_recv, hop_send, hop_recv,
-    group_send, group_recv, far_send, far_recv, sum_send, sum_recv, x_send, x_recv, ready,
+    left_send, left_recv, right_send, right_recv, pass_send, pass_recv,
+    group_send, group_recv, far_send, far_recv, sum_send, sum_recv, x_send, x_recv, first_send, first_recv, ready,
 ):
     section = lax.axis_index("section")
     et = lax.axis_index("et")
@@ -88,7 +89,7 @@
 
     barrier = pltpu.get_barrier_semaphore()
     near = [x_peer] + [at_y(k) for k in (1, 3)] + [at_z(k) for k in (1, 3)]
-    peers = [pair, sibling] + near
+    peers = [pair, sibling, at_y(2), at_z(2)] + near
     for peer in peers:
         pl.semaphore_signal(barrier, inc=1, device_id=peer, device_id_type=MESH)
     pl.semaphore_wait(barrier, len(peers))
@@ -113,6 +114,59 @@
     along = lax.broadcasted_iota(jnp.int32, (tok, slots_n), 0)
     place = [jnp.where(slots_ref[0] == along + o, 1.0, 0.0).astype(BF) for o in offsets]
 
+    def turn(rows, into):
+        for b in range(width // 128):
+            block = rows[:, b * 128:(b + 1) * 128].astype(F32)
+            into[b // 4, b % 4] = block.T.astype(BF)
+
+    def deal_copies(which):
+        source = (x_turned, s_turned)[which]
+        copies = []
+        for h in range(2):
+            for k, step in ((2, 2), (1, step_a), (3, step_b)):
+                there = (gather_pos[h] + step) % RING
+                share = source.at[:, there] if h == 0 else source.at[there]
+                copies.append(remote(share, left.at[which, h, :, :, pl.ds(k * 128, 128)],
+                                     left_send.at[which, h, k - 1], left_recv.at[which, h, k - 1],
+                                     gather_to[h](step)))
+        return copies
+
+    def deal(which):
+        source = (x_turned, s_turned)[which]
+        left[which, 0, :, :, 0:128] = source[:, gather_pos[0]]
+        left[which, 1, :, :, 0:128] = source[gather_pos[1]]
+        for copy in deal_copies(which):
+            copy.start()
+
+    def right_piece(t, h, p, k):
+        start, count = part_of[p]
+        return right.at[t, pl.ds(half * h + start, count), pl.ds(k * slots_n, slots_n), :]
+
+    def right_copy(t, h, d, p):
+        return remote(right_piece(t, h, p, 0), right_piece(t, h, p, 1 + 2 * d),
+                      right_send.at[t, h, d, p], right_recv.at[t, h, d, p], gather_to[h](steps[d]))
+
+    def right_pass(t, h, d):
+        return remote(right_piece(t, h, d, 1 + 2 * d), right_piece(t, h, d, 2),
+                      pass_send.at[t, h, d], pass_recv.at[t, h, d], gather_to[h](steps[d]))
+
+    def right_spread(t):
+        for d, p in ((0, 0), (1, 1), (0, 1), (1, 0)):
+            for h in range(2):
+                right_copy(t, h, d, p).start()
+
+    def right_pass_on(t):
+        for h in range(2):
+            for d in range(2):
+                right_copy(t, h, d, d).wait_recv()
+                right_pass(t, h, d).start()
+
+    def right_wait(t):
+        for h in range(2):
+            for d in range(2):
+                right_copy(t, h, d, 1 - d).wait_recv()
+                right_pass(t, h, d).wait_recv()
+
     groups = (x_group, s_group)
     span = width // 2
 
@@ -128,13 +182,9 @@
                       far_send.at[which, h, d], far_recv.at[which, h, d], gather_to[h](steps[d]))
 
     def spread(which):
-        copies = []
         for d, p in ((0, 0), (1, 1), (0, 1), (1, 0)):
             for h in range(2):
-                copy = spread_copy(which, h, d, p)
-                copy.start()
-                copies.append(copy)
-        return copies
+                spread_copy(which, h, d, p).start()
 
     def pass_on(which):
         for h in range(2):
@@ -147,6 +197,15 @@
             for d in range(2):
                 spread_copy(which, h, d, 1 - d).wait_recv()
                 pass_copy(which, h, d).wait_recv()
+
+    def left_make(which):
+        for h in range(2):
+            for j in range(RING):
+                at = (j * RING + gather_pos[h]) if h == 0 else (gather_pos[h] * RING + j)
+                cols = pl.ds(pl.multiple_of(at * 128, 128), 128)
+                for k in range(RING):
+                    tile = groups[which][h, k * slots_n:(k + 1) * slots_n, cols].astype(F32)
+                    left[which, h, j, :, k * slots_n:(k + 1) * slots_n] = tile.T.astype(BF)
 
     own = pl.ds(0, slots_n)
     others = pl.ds(slots_n, (RING - 1) * slots_n)
@@ -175,7 +234,7 @@
         return w_load(w2_hbm, w2.at[i % ring_w2], i % chunks, w2_sem.at[i % ring_w2])
 
     def w2_next(i):
-        @pl.when(i + ring_w2 < 2 * chunks)
+        @pl.when(i + ring_w2 < (2 - section) * chunks)
         def _():
             w2_load(i + ring_w2).start()
 
@@ -184,7 +243,13 @@
     picked = (dot(pick[0], x_full[0]) + dot(pick[1], x_full[1])).astype(BF)
     for h in range(2):
         x_group[h, own, :] = picked
-    sent = spread(0)
+    @pl.when(section == 0)
+    def _():
+        spread(0)
+
+    @pl.when(section == 1)
+    def _():
+        turn(x_group.at[0, own], x_turned)
 
     @pl.loop(0, chunks)
     def _(c):
@@ -192,8 +257,6 @@
         w_load(w3_hbm, w3.at[c], c, load_sem.at[1, c]).wait()
         forward(c, x_group[0, own, :], own)
 
-    pass_on(0)
-
     blocks = grads_both.shape[0]
     step = width // blocks
 
@@ -203,12 +266,15 @@
 
     @pl.when(section == 1)
     def _():
+        right_spread(0)
         g_load.wait()
         g_swap.wait_recv()
 
     @pl.when(section == 0)
     def _():
+        pass_on(0)
         forward_others()
+        left_make(0)
 
     gate_block = down_rows(gates_ref[0])
     gates = jnp.concatenate([gate_block] * (COLS // 128), axis=1)
@@ -225,7 +291,10 @@
         for h in range(2):
             s_group[h, own, cols] = scaled_rows
 
-    sent += spread(1)
+    @pl.when(section == 0)
+    def _():
+        spread(1)
+
     value_mine[...] = jnp.zeros_like(value_mine)
 
     @pl.loop(0, chunks)
@@ -236,6 +305,11 @@
         product = right[0, c, own, :].astype(F32) * back
         value_mine[...] += product[:, :128] + product[:, 128:]
         backward(c, gates * back, own)
+
+    @pl.when(section == 1)
+    def _():
+        right_spread(1)
+        right_spread(2)
 
     value_swap = remote(value_mine, value_theirs, pair_send.at[2], pair_recv.at[2], pair)
     value_swap.start()
@@ -253,36 +327,33 @@
         rows_mine[b] = total_rows.astype(BF)
         rows_swap(b).start()
 
-    pass_on(1)
-
-    for b in range(blocks):
+        @pl.when((section == 0) & (b == 1))
+        def _():
+            pass_on(1)
+
+    @pl.when(section == 1)
+    def _():
+        right_pass_on(0)
+        turn(s_group.at[0, own], s_turned)
+        deal(1)
+        deal(0)
+
+    def token_grads(b, halves):
         rows_swap(b).wait_recv()
         cols = slice(b * step, (b + 1) * step)
-
-        def token_grads(i):
+        for i in halves:
             added = dot_nt(place[i], rows_mine[b]) + dot_nt(place[i], rows_theirs[b])
             grads_both[b, i] = (g_full[i, :, cols].astype(F32) + added).astype(BF)
-
-        token_grads(0)
-
-        @pl.when(section == 1)
-        def _():
-            token_grads(1)
+        in_grad[0, 0, :, cols] = grads_both[b, 0]
+
+    @pl.when(section == 1)
+    def _():
+        for b in range(blocks):
+            token_grads(b, (0, 1))
             hop(b).start()
-
-        in_grad[0, 0, :, cols] = grads_both[b, 0]
 
     outs = (down_out, gate_out, up_out)
     block = RING * 128
-
-    def left_make(which):
-        for h in range(2):
-            for j in range(RING):
-                at = (j * RING + gather_pos[h]) if h == 0 else (gather_pos[h] * RING + j)
-                cols = pl.ds(pl.multiple_of(at * 128, 128), 128)
-                for k in range(RING):
-                    tile = groups[which][h, k * slots_n:(k + 1) * slots_n, cols].astype(F32)
-                    left[which, h, j * 128:(j + 1) * 128, k * slots_n:(k + 1) * slots_n] = tile.T.astype(BF)
 
     def multiply(t, h):
         which = 1 if t == 0 else 0
@@ -290,122 +361,240 @@
         @pl.loop(0, half)
         def _(n):
             c = half * h + n
-            w1[c, t * block:(t + 1) * block, :] = dot(left[which, h], right[t, c]).astype(BF)
-
-    def part_at(t, h, p, row):
+            w1[c, t * block:(t + 1) * block, :] = dot(left[which, h].reshape(block, RING * slots_n), right[t, c]).astype(BF)
+
+    def rows_at(t, row, side, early):
+        count = 64 if early else 128
+        at = t * block + row * 128 + (side * 64 if early else 0)
+        return pl.ds(pl.multiple_of(at, 64), count)
+
+    def part_at(t, h, p, row, early):
         start, count = part_of[p]
-        return (pl.ds(half * h + start, count), pl.ds(pl.multiple_of(t * block + row * 128, 128), 128), slice(None))
-
-    def of_block(t, h, p, step):
-        return part_at(t, h, p, (reduce_pos[h] + step) % RING)
-
-    def far_sum(t, h, d):
-        return remote(w1.at[of_block(t, h, d, 2)], w3.at[part_at(t, h, d, 2)],
+        return (pl.ds(half * h + start, count), rows_at(t, row, 0, early), slice(None))
+
+    def of_block(t, h, p, step, early):
+        start, count = part_of[p]
+        return (pl.ds(half * h + start, count), rows_at(t, (reduce_pos[h] + step) % RING, x, early), slice(None))
+
+    def first_sum(h, j):
+        cols = pl.ds(half * h, half)
+        return remote(w1.at[cols, pl.ds(pl.multiple_of(j * 128 + (1 - x) * 64, 64), 64), :],
+                      w3.at[cols, pl.ds(j * 128 + 64, 64), :], first_send.at[h, j], first_recv.at[h, j], x_peer)
+
+    def first_start(h):
+        for j in range(RING):
+            first_sum(h, j).start()
+
+    def first_end(h):
+        for j in range(RING):
+            first_sum(h, j).wait_recv()
+            cols = pl.ds(half * h, half)
+            mine = (cols, pl.ds(pl.multiple_of(j * 128 + x * 64, 64), 64), slice(None))
+            theirs = (cols, pl.ds(j * 128 + 64, 64), slice(None))
+            w1[mine] = (w1[mine].astype(F32) + w3[theirs].astype(F32)).astype(BF)
+
+    def far_sum(t, h, d, early):
+        return remote(w1.at[of_block(t, h, d, 2, early)], w3.at[part_at(t, h, d, 2, early)],
                       sum_send.at[t, h, 0, d], sum_recv.at[t, h, 0, d], reduce_to[h](steps[d]))
 
-    def near_sum(t, h, d, p):
-        return remote(w1.at[of_block(t, h, p, steps[d])], w3.at[part_at(t, h, p, 1 + 2 * d)],
+    def near_sum(t, h, d, p, early):
+        return remote(w1.at[of_block(t, h, p, steps[d], early)], w3.at[part_at(t, h, p, 1 + 2 * d, early)],
                       sum_send.at[t, h, 1 + p, d], sum_recv.at[t, h, 1 + p, d], reduce_to[h](steps[d]))
 
-    def reduce_start(t, h):
-        copies = [far_sum(t, h, d) for d in range(2)] + [near_sum(t, h, d, 1 - d) for d in range(2)]
-        for copy in copies:
-            copy.start()
-        return copies
-
-    def merge(t, h):
-        copies = []
+    def reduce_start(t, h, early=False):
         for d in range(2):
-            far_sum(t, h, d).wait_recv()
-            here = of_block(t, h, d, steps[d])
-            w1[here] = (w1[here].astype(F32) + w3[part_at(t, h, d, 2)].astype(F32)).astype(BF)
-            copy = near_sum(t, h, d, d)
-            copy.start()
-            copies.append(copy)
-        return copies
-
-    def total(t, h, c, side):
+            far_sum(t, h, d, early).start()
+        for d in range(2):
+            near_sum(t, h, d, 1 - d, early).start()
+
+    def merge(t, h, early=False):
+        for d in range(2):
+            far_sum(t, h, d, early).wait_recv()
+            here = of_block(t, h, d, steps[d], early)
+            w1[here] = (w1[here].astype(F32) + w3[part_at(t, h, d, 2, early)].astype(F32)).astype(BF)
+            near_sum(t, h, d, d, early).start()
+
+    def reduce_sent(t, h, early=False):
+        for d in range(2):
+            far_sum(t, h, d, early).wait_send()
+            for p in range(2):
+                near_sum(t, h, d, p, early).wait_send()
+            if not early:
+                x_copy(t, h, d).wait_send()
+
+    def total(t, h, c, side, early):
         here = pl.multiple_of(t * block + reduce_pos[h] * 128 + side * 64, 64)
         value = w1[c, pl.ds(here, 64), :].astype(F32)
         for k in (1, 3):
-            there = pl.multiple_of(t * block + k * 128 + side * 64, 64)
+            there = pl.multiple_of(t * block + k * 128 + (0 if early else side * 64), 64)
             value = value + w3[c, pl.ds(there, 64), :].astype(F32)
         return value
 
-    def x_copy(t, h):
-        at = (pl.ds(half * h, half), pl.ds(3 * block + t * 64, 64), slice(None))
-        return remote(w1.at[at], w3.at[at], x_send.at[t, h], x_recv.at[t, h], x_peer)
+    def x_copy(t, h, p):
+        start, count = part_of[p]
+        at = (pl.ds(half * h + start, count), pl.ds(3 * block + t * 64, 64), slice(None))
+        return remote(w1.at[at], w3.at[at], x_send.at[t, h, p], x_recv.at[t, h, p], x_peer)
+
+    def near_wait(t, h, p, early):
+        for d in range(2):
+            near_sum(t, h, d, p, early).wait_recv()
 
     def reduce_end(t, h):
-        for d in range(2):
-            for p in range(2):
-                near_sum(t, h, d, p).wait_recv()
-
-        @pl.loop(0, half)
-        def _(n):
-            c = half * h + n
-            w1[c, 3 * block + t * 64:3 * block + (t + 1) * 64, :] = total(t, h, c, 1 - x).astype(BF)
-        copy = x_copy(t, h)
-        copy.start()
-        return [copy]
-
-    def finish(t, h):
-        x_copy(t, h).wait_recv()
-        for n in range(half):
-            c = half * h + n
-            arrived = w3[c, 3 * block + t * 64:3 * block + (t + 1) * 64, :].astype(F32)
-            outs[t][0, :, c * COLS:(c + 1) * COLS] = ((total(t, h, c, x) + arrived) * (1.0 / 32.0)).astype(BF)
-
-    @pl.when(section == 1)
-    def _():
-        forward_others()
+        for p in range(2):
+            near_wait(t, h, p, False)
+            start, count = part_of[p]
+
+            @pl.loop(0, count)
+            def _(n):
+                c = half * h + start + n
+                w1[c, 3 * block + t * 64:3 * block + (t + 1) * 64, :] = total(t, h, c, 1 - x, False).astype(BF)
+            x_copy(t, h, p).start()
+
+    def finish(t, h, early=False):
+        for p in range(2):
+            if early:
+                near_wait(t, h, p, True)
+            else:
+                x_copy(t, h, p).wait_recv()
+            start, count = part_of[p]
+            for n in range(start, start + count):
+                c = half * h + n
+                value = total(t, h, c, x, early)
+                if not early:
+                    value = value + w3[c, 3 * block + t * 64:3 * block + (t + 1) * 64, :].astype(F32)
+                outs[t][0, :, c * COLS:(c + 1) * COLS] = (value * (1.0 / 32.0)).astype(BF)
 
     for peer in near:
         pl.semaphore_signal(ready, inc=1, device_id=peer, device_id_type=MESH)
-    group_wait(1)
-    left_make(1)
+
+    @pl.when(section == 0)
+    def _():
+        group_wait(1)
+        left_make(1)
+
+    @pl.when(section == 1)
+    def _():
+        right_pass_on(1)
+        for copy in deal_copies(1):
+            copy.wait_recv()
+        right_wait(0)
+
     multiply(0, 0)
     pl.semaphore_wait(ready, len(near))
-    sent += reduce_start(0, 0)
+
+    @pl.when(section == 0)
+    def _():
+        reduce_start(0, 0)
+
+    @pl.when(section == 1)
+    def _():
+        first_start(0)
+        right_pass_on(2)
+
     multiply(0, 1)
-    sent += reduce_start(0, 1)
-
-    @pl.loop(0, chunks)
-    def _(c):
-        i = chunks + c
-        w2_load(i).wait()
-        scaled = dot(s_group[c // half, others, :], w2[i % ring_w2])
-        w2_next(i)
-        backward(c, scaled, others)
-
-    left_make(0)
-    for t in (1, 2):
-        for h in range(2):
-            multiply(t, h)
-            sent += reduce_start(t, h)
-            sent += merge(t - 1, h)
+
+    @pl.when(section == 0)
+    def _():
+        reduce_start(0, 1)
+
+        @pl.loop(0, chunks)
+        def _(c):
+            i = chunks + c
+            w2_load(i).wait()
+            scaled = dot(s_group[c // half, others, :], w2[i % ring_w2])
+            w2_next(i)
+            backward(c, scaled, others)
+
+    @pl.when(section == 1)
+    def _():
+        first_start(1)
+        for copy in deal_copies(0):
+            copy.wait_recv()
+        right_wait(1)
+
+    multiply(1, 0)
+    reduce_start(1, 0)
+
+    @pl.when(section == 0)
+    def _():
+        merge(0, 0)
+
+    multiply(1, 1)
+    reduce_start(1, 1)
+
+    @pl.when(section == 0)
+    def _():
+        merge(0, 1)
+
+    @pl.when(section == 1)
+    def _():
+        right_wait(2)
+
     for h in range(2):
-        sent += reduce_end(0, h)
+        multiply(2, h)
+        reduce_start(2, h)
+        merge(1, h)
+
+    @pl.when(section == 0)
+    def _():
+        for h in range(2):
+            reduce_end(0, h)
+        for b in range(blocks):
+            token_grads(b, (0,))
+
     for h in range(2):
-        sent += merge(2, h)
+        merge(2, h)
+
+    @pl.when(section == 1)
+    def _():
+        for h in range(2):
+            first_end(h)
+            reduce_start(0, h, True)
+
     for h in range(2):
-        sent += reduce_end(1, h)
+        reduce_end(1, h)
+
+    @pl.when(section == 1)
+    def _():
+        for h in range(2):
+            merge(0, h, True)
+
     value_swap.wait_recv()
     value_out[0] = jnp.sum((value_mine[...] + value_theirs[...]).T, axis=0, keepdims=True)
+
+    @pl.when(section == 0)
+    def _():
+        for h in range(2):
+            finish(0, h)
+
     for h in range(2):
-        finish(0, h)
-    for h in range(2):
-        sent += reduce_end(2, h)
+        reduce_end(2, h)
+
+    @pl.when(section == 1)
+    def _():
+        for h in range(2):
+            finish(0, h, True)
+
     for t in (1, 2):
         for h in range(2):
             finish(t, h)
 
-    for copy in sent:
-        copy.wait_send()
-    for which in range(2):
-        for h in range(2):
-            for d in range(2):
-                pass_copy(which, h, d).wait_send()
+    for t in (1, 2):
+        for h in range(2):
+            reduce_sent(t, h)
+
+    @pl.when(section == 0)
+    def _():
+        for h in range(2):
+            reduce_sent(0, h)
+
+    @pl.when(section == 1)
+    def _():
+        for h in range(2):
+            reduce_sent(0, h, True)
+            for j in range(RING):
+                first_sum(h, j).wait_send()
+
     for b in range(blocks):
         rows_swap(b).wait_send()
     value_swap.wait_send()
@@ -413,10 +602,24 @@
     @pl.when(section == 0)
     def _():
         x_swap.wait_send()
+        for which in range(2):
+            for h in range(2):
+                for d in range(2):
+                    pass_copy(which, h, d).wait_send()
+                    for p in range(2):
+                        spread_copy(which, h, d, p).wait_send()
 
     @pl.when(section == 1)
     def _():
         g_swap.wait_send()
+        for copy in deal_copies(0) + deal_copies(1):
+            copy.wait_send()
+        for t in range(3):
+            for h in range(2):
+                for d in range(2):
+                    right_pass(t, h, d).wait_send()
+                    for p in range(2):
+                        right_copy(t, h, d, p).wait_send()
         for b in range(blocks):
             hop(b).wait_send()
 
@@ -458,8 +661,10 @@
             pltpu.VMEM((slots_n, width), BF),
             pltpu.VMEM((2, RING * slots_n, width), BF),
             pltpu.VMEM((2, RING * slots_n, width), BF),
+            pltpu.VMEM((RING, RING, 128, slots_n), BF),
+            pltpu.VMEM((RING, RING, 128, slots_n), BF),
             pltpu.VMEM((3, chunks, RING * slots_n, COLS), BF),
-            pltpu.VMEM((2, 2, RING * 128, RING * slots_n), BF),
+            pltpu.VMEM((2, 2, RING, 128, RING * slots_n), BF),
             pltpu.VMEM((4, width // 4, slots_n), BF),
             pltpu.VMEM((4, width // 4, slots_n), BF),
             pltpu.VMEM((4, 2, tok, width // 4), BF),
@@ -467,8 +672,10 @@
             pltpu.VMEM((slots_n, 128), F32),
             sem((2, chunks)), sem((W2_RING,)), sem((2,)),
             sem((3,)), sem((3,)), sem((4,)), sem((4,)), sem((4,)), sem((4,)),
+            sem((2, 2, 3)), sem((2, 2, 3)), sem((3, 2, 2, 2)), sem((3, 2, 2, 2)), sem((3, 2, 2)), sem((3, 2, 2)),
             sem((2, 2, 2, 2)), sem((2, 2, 2, 2)), sem((2, 2, 2)), sem((2, 2, 2)),
-            sem((3, 2, 3, 2)), sem((3, 2, 3, 2)), sem((3, 2)), sem((3, 2)),
+            sem((3, 2, 3, 2)), sem((3, 2, 3, 2)), sem((3, 2, 2)), sem((3, 2, 2)),
+            sem((2, RING)), sem((2, RING)),
             pltpu.SemaphoreType.REGULAR,
         ],
         compiler_params=pltpu.CompilerParams(

time: 133 us -> 128 us (0.962)
  Pallas kernels: 132 us -> 127 us
    pallas_call x1, Pallas kernels: 129 us -> 125 us  [per_device(): pl.pallas_call(body, out_shape=shapes, in_specs=[vmem, vmem, hbm, hbm, hb...]
where the time goes in v3:
time: 128 us
  Pallas kernels  127 us (99%)
    pallas_call x1, Pallas kernels, per_device(): pl.pallas_call(body, out_shape=shapes, in_specs=[vmem, vmem, hbm, hbm, hb...  125 us
    pallas_call x1, Pallas kernels, per_device(): pl.pallas_call(hand_out, out_shape=shapes, in_specs=[vmem] * 5, out_specs...  2.74 us

profile of v3, /device:TPU:0, one launch (start us, length us, event | category | flops | bytes accessed | tf_op | source)
XLA Modules:
  0.0 128.1 jit_solution(1742765673767124952)
XLA Ops:
  0.6 124.7 %shard_map.110 = (bf16[1,1,128,2048]{3,2,1,0:T(8,128)(2,1)}, bf16[1,64,3584]{2,1,0:T(8,128)(2,1)}, bf16[1,64,3584]{2,1,0:T(8,128)(2,1)}, bf16[1,64,3584]{2,1,0:T(8,128)(2,1)}, f32[1,1,128]{2,1,0:T(1,128)}) custom-call(s32[1,1,128]{2,1,0:T(1,128)} %slots_ref.1, f32[1,1,128]{2,1,0:T(1,128)} %gates_ref.1, bf16[1,1,128,2048]{3,2,1,0:T(8,128)(2,1)} %x_hbm.1, ...), custom_call_target="tpu_custom_call" | custom-call | tf_op jit(solution)/shard_map/pallas_call | solution.py:650
  125.4 2.7 %shard_map.111 = (bf16[1,1,128,2048]{3,2,1,0:T(8,128)(2,1)}, bf16[1,64,3584]{2,1,0:T(8,128)(2,1)}, bf16[1,64,3584]{2,1,0:T(8,128)(2,1)}, bf16[1,64,3584]{2,1,0:T(8,128)(2,1)}, f32[1,1,128]{2,1,0:T(1,128)}) custom-call(bf16[1,1,128,2048]{3,2,1,0:T(8,128)(2,1)} %get-tuple-element.10.refs_0_, bf16[1,64,3584]{2,1,0:T(8,128)(2,1)} %get-tuple-element.11.refs_1_, ...), custom_call_target="tpu_custom_call" | custom-call | tf_op jit(solution)/shard_map/pallas_call | solution.py:684

commit v4 on v3

--- a/solution.py
+++ b/solution.py
@@ -70,28 +70,29 @@
         start = pl.multiple_of(c * COLS, COLS)
         return pltpu.make_async_copy(hbm.at[0, :, pl.ds(start, COLS)], ref, sem)
 
-    x_load = pltpu.make_async_copy(x_hbm.at[0, 0], x_full.at[0], local_sem.at[0])
-    g_load = pltpu.make_async_copy(g_hbm.at[0], g_full.at[0], local_sem.at[1])
-    x_load.start()
-
-    @pl.when(section == 1)
-    def _():
-        g_load.start()
-
-    @pl.loop(0, chunks)
-    def _(c):
-        w_load(w1_hbm, w1.at[c], c, load_sem.at[0, c]).start()
-        w_load(w3_hbm, w3.at[c], c, load_sem.at[1, c]).start()
-
-    @pl.loop(0, ring_w2)
-    def _(c):
-        w_load(w2_hbm, w2.at[c], c, w2_sem.at[c]).start()
-
     barrier = pltpu.get_barrier_semaphore()
     near = [x_peer] + [at_y(k) for k in (1, 3)] + [at_z(k) for k in (1, 3)]
     peers = [pair, sibling, at_y(2), at_z(2)] + near
     for peer in peers:
         pl.semaphore_signal(barrier, inc=1, device_id=peer, device_id_type=MESH)
+
+    x_load = pltpu.make_async_copy(x_hbm.at[0, 0], x_full.at[0], local_sem.at[0])
+    g_load = pltpu.make_async_copy(g_hbm.at[0], g_full.at[0], local_sem.at[1])
+    x_load.start()
+
+    @pl.when(section == 1)
+    def _():
+        g_load.start()
+
+    @pl.loop(0, chunks)
+    def _(c):
+        w_load(w1_hbm, w1.at[c], c, load_sem.at[0, c]).start()
+        w_load(w3_hbm, w3.at[c], c, load_sem.at[1, c]).start()
+
+    @pl.loop(0, ring_w2)
+    def _(c):
+        w_load(w2_hbm, w2.at[c], c, w2_sem.at[c]).start()
+
     pl.semaphore_wait(barrier, len(peers))
 
     x_swap = remote(x_hbm.at[0, 0], x_full.at[1], pair_send.at[0], pair_recv.at[0], pair)
@@ -294,6 +295,12 @@
     @pl.when(section == 0)
     def _():
         spread(1)
+
+    @pl.when(section == 1)
+    def _():
+        turn(s_group.at[0, own], s_turned)
+        deal(1)
+        deal(0)
 
     value_mine[...] = jnp.zeros_like(value_mine)
 
@@ -331,13 +338,6 @@
         def _():
             pass_on(1)
 
-    @pl.when(section == 1)
-    def _():
-        right_pass_on(0)
-        turn(s_group.at[0, own], s_turned)
-        deal(1)
-        deal(0)
-
     def token_grads(b, halves):
         rows_swap(b).wait_recv()
         cols = slice(b * step, (b + 1) * step)
@@ -351,6 +351,10 @@
         for b in range(blocks):
             token_grads(b, (0, 1))
             hop(b).start()
+
+    @pl.when(section == 1)
+    def _():
+        right_pass_on(0)
 
     outs = (down_out, gate_out, up_out)
     block = RING * 128

time: 128 us -> 128 us (level)
  no operation moved by 1% of the time
where the time goes in v4:
time: 128 us
  Pallas kernels  127 us (99%)
    pallas_call x1, Pallas kernels, per_device(): pl.pallas_call(body, out_shape=shapes, in_specs=[vmem, vmem, hbm, hbm, hb...  124 us
    pallas_call x1, Pallas kernels, per_device(): pl.pallas_call(hand_out, out_shape=shapes, in_specs=[vmem] * 5, out_specs...  2.74 us

profile of v4, /device:TPU:0, one launch (start us, length us, event | category | flops | bytes accessed | tf_op | source)
XLA Modules:
  0.0 127.9 jit_solution(9692369791252564012)
XLA Ops:
  0.6 124.5 %shard_map.110 = (bf16[1,1,128,2048]{3,2,1,0:T(8,128)(2,1)}, bf16[1,64,3584]{2,1,0:T(8,128)(2,1)}, bf16[1,64,3584]{2,1,0:T(8,128)(2,1)}, bf16[1,64,3584]{2,1,0:T(8,128)(2,1)}, f32[1,1,128]{2,1,0:T(1,128)}) custom-call(s32[1,1,128]{2,1,0:T(1,128)} %slots_ref.1, f32[1,1,128]{2,1,0:T(1,128)} %gates_ref.1, bf16[1,1,128,2048]{3,2,1,0:T(8,128)(2,1)} %x_hbm.1, ...), custom_call_target="tpu_custom_call" | custom-call | tf_op jit(solution)/shard_map/pallas_call | solution.py:654
  125.1 2.7 %shard_map.111 = (bf16[1,1,128,2048]{3,2,1,0:T(8,128)(2,1)}, bf16[1,64,3584]{2,1,0:T(8,128)(2,1)}, bf16[1,64,3584]{2,1,0:T(8,128)(2,1)}, bf16[1,64,3584]{2,1,0:T(8,128)(2,1)}, f32[1,1,128]{2,1,0:T(1,128)}) custom-call(bf16[1,1,128,2048]{3,2,1,0:T(8,128)(2,1)} %get-tuple-element.10.refs_0_, bf16[1,64,3584]{2,1,0:T(8,128)(2,1)} %get-tuple-element.11.refs_1_, ...), custom_call_target="tpu_custom_call" | custom-call | tf_op jit(solution)/shard_map/pallas_call | solution.py:688
